TPU v7x, 32 devices: a whole 2x2x4 slice. The times are simulated.
32 devices in a mesh: dp: 8 (over z, x), owner: 4 (over y, core).
Axes of the slice: x: 2, y: 2, z: 4, core: 2. Of those that a mesh axis runs over, the one named last changes fastest.
Arguments:
- grads: bfloat16 [8, 10, 1024, 1024], P('dp', None, None, 'owner'), may hold values from -0.059814453 to 0.059814453
- owner_of: int32 [10], replicated, may hold values from 0 to 3, as said below
- left_stats: float32 [4, 6, 1024, 1024], P('owner', None, 'dp'), may hold values from -6 to 6
- right_stats: float32 [4, 6, 1024, 1024], P('owner', None, 'dp'), may hold values from -6 to 6
- left_root: bfloat16 [4, 6, 1024, 1024], P('owner', None, 'dp'), as said below
- right_root: bfloat16 [4, 6, 1024, 1024], P('owner', None, 'dp'), as said below
- weights: bfloat16 [4, 6, 1024, 1024], P('owner', None, 'dp'), may hold values from -6 to 6
- first_moment: float32 [4, 6, 1024, 1024], P('owner', None, 'dp'), may hold values from -3 to 3
- second_moment: float32 [4, 6, 1024, 1024], P('owner', None, 'dp'), may hold values from 0.0001 to 0.01
Outputs:
- new_left: float32 [4, 6, 1024, 1024], P('owner', None, 'dp')
- new_right: float32 [4, 6, 1024, 1024], P('owner', None, 'dp')
- new_first: float32 [4, 6, 1024, 1024], P('owner', None, 'dp')
- new_second: float32 [4, 6, 1024, 1024], P('owner', None, 'dp')
- new_weights: bfloat16 [10, 1024, 1024], P(None, None, 'owner')
Inputs may be any that keep to these rules, and one draw needn't show every extreme that they name: `owner_of`: no owner holds more than 6 blocks, and one owner holds exactly 6. `left_root`: Symmetric. `right_root`: Symmetric.
All inputs are finite; a program needn't handle non-finite values.
Results may differ from a plain program's by a relative error of at most 0.012.
Values may be sent and summed in bfloat16 or wider, within the bound.
A program may use at most 192 MiB of HBM per device.

v0:
```python
import jax
import jax.numpy as jnp
from jax import lax
from jax.sharding import PartitionSpec as P


def slot_table(owner_of):
    count = owner_of.shape[0]
    here = lax.broadcasted_iota(jnp.int32, (count, count), 0)
    prior = lax.broadcasted_iota(jnp.int32, (count, count), 1)
    same = (owner_of[:, None] == owner_of[None, :]) & (prior < here)
    return jnp.sum(same.astype(jnp.int32), axis=1)


def precondition(rounded, left_rows, right_rows):
    rows, width = rounded.shape
    first_row = lax.axis_index("dp") * rows
    piece = lax.all_gather(rounded, "dp", axis=0, tiled=True)
    block = lax.dot_general(
        rounded, piece, (((1,), (1,)), ((), ())), preferred_element_type=jnp.float32
    )
    left_part = block
    own_cols = lax.dynamic_slice_in_dim(piece, first_row, rows, 1)
    right_part = lax.dot_general(
        own_cols, piece, (((0,), (0,)), ((), ())), preferred_element_type=jnp.float32
    )
    half_part = jnp.dot(left_rows, piece, preferred_element_type=jnp.float32)
    left_part, right_part, half_part = (left_part, right_part, half_part)
    half = half_part.astype(jnp.bfloat16)
    direction = jnp.dot(
        half,
        lax.all_gather(right_rows, "dp", axis=0, tiled=True),
        preferred_element_type=jnp.float32,
    )
    return (left_part, right_part, direction)


def per_device(
    grads,
    owner_of,
    left_stats,
    right_stats,
    left_root,
    right_root,
    weights,
    first_moment,
    second_moment,
):
    owners = lax.axis_size("owner")
    slots = left_stats.shape[1]
    rows = left_stats.shape[2]
    count = owner_of.shape[0]
    slot_of = slot_table(owner_of)
    targets = owner_of * slots + slot_of
    reduced = lax.psum_scatter(
        grads[0].astype(jnp.float32).astype(jnp.bfloat16), "dp", scatter_dimension=1, tiled=True
    ).astype(jnp.float32)
    columns = reduced.shape[2]
    place_at = lax.broadcasted_iota(jnp.int32, (owners * slots, count), 0)
    place = (targets[None, :] == place_at).astype(jnp.float32)
    outgoing = jnp.einsum("km,mrc->krc", place, reduced, precision=lax.Precision.HIGHEST)
    outgoing = outgoing.reshape((owners, slots, rows, columns))
    owned = lax.all_to_all(
        outgoing.astype(jnp.bfloat16), "owner", split_axis=0, concat_axis=3, tiled=True
    ).astype(outgoing.dtype)[0]
    rounded = owned.astype(jnp.bfloat16)
    results = [
        precondition(rounded[slot], left_root[0, slot], right_root[0, slot])
        for slot in range(slots)
    ]
    left_inc = jnp.stack([item[0] for item in results])
    right_inc = jnp.stack([item[1] for item in results])
    direction = jnp.stack([item[2] for item in results])
    new_left = 0.95 * left_stats[0] + left_inc
    new_right = 0.95 * right_stats[0] + right_inc
    new_first = 0.9 * first_moment[0] + 0.1 * owned
    new_second = 0.999 * second_moment[0] + 0.001 * owned * owned
    adam = new_first / (jnp.sqrt(new_second) + 1e-08)
    adam_total, dir_total = lax.psum(
        (jnp.sum(adam * adam, axis=(1, 2)), jnp.sum(direction * direction, axis=(1, 2))), "dp"
    )
    graft = jnp.sqrt(adam_total) / jnp.sqrt(dir_total + 1e-12)
    moved = weights[0].astype(jnp.float32) - 0.1 * graft[:, None, None] * direction
    updated = moved * lax.rsqrt(jnp.mean(moved * moved, axis=-1, keepdims=True) + 1e-06)
    finished = updated.astype(jnp.bfloat16)
    by_columns = lax.all_to_all(finished, "owner", split_axis=2, concat_axis=0, tiled=True)
    picked = jnp.take(by_columns, targets, axis=0)
    new_weights = lax.all_gather(picked, "dp", axis=1, tiled=True)
    return (new_left[None], new_right[None], new_first[None], new_second[None], new_weights)


def solution(mesh):
    placed = (
        P("dp", None, None, "owner"),
        P(),
        P("owner", None, "dp", None),
        P("owner", None, "dp", None),
        P("owner", None, "dp", None),
        P("owner", None, "dp", None),
        P("owner", None, "dp", None),
        P("owner", None, "dp", None),
        P("owner", None, "dp", None),
    )
    return jax.shard_map(
        per_device,
        mesh=mesh,
        in_specs=placed,
        out_specs=(
            P("owner", None, "dp", None),
            P("owner", None, "dp", None),
            P("owner", None, "dp", None),
            P("owner", None, "dp", None),
            P(None, None, "owner"),
        ),
        check_vma=False,
    )
```

profile of v0, /device:TPU:0, one launch (start us, length us, event | category | flops | bytes accessed | tf_op | source)
XLA Modules:
  0.0 888.4 jit_solution(14392031060074100104)
XLA Ops:
  10.1 107.2 %reduce-scatter.2.cloned.1.call-done = bf16[10,128,256]{2,1,0:T(8,128)(2,1)} async-done(((bf16[10,1024,256]{2,1,0:T(8,128)(2,1)}), bf16[10,128,256]{2,1,0:T(8,128)(2,1)}) %reduce-scatter.2.cloned.1.call-update) | async-done | bytes 655376 | tf_op jit(solution)/shard_map/reduce_scatter | solution.py:55
  119.5 22.6 %all_to_all.33 = bf16[4,6,128,256]{3,2,1,0:T(8,128)(2,1)S(1)} all-to-all(bf16[4,6,128,256]{3,2,1,0:T(8,128)(2,1)S(1)} %bitcast.204), channel_id=1, replica_groups=mesh['dp'=8,'owner'=4] {'owner'}, dimensions={0} | all-to-all | bytes 3145728 | tf_op jit(solution)/shard_map/all_to_all | solution.py:63
  154.4 4.7 copy.83
  166.1 4.9 fusion.7
  171.0 49.2 %all-gather.20.cloned.1.call-done = bf16[1024,1024]{0,1:T(8,128)(2,1)} async-done(((bf16[128,1024]{0,1:T(8,128)(2,1)}), bf16[1024,1024]{0,1:T(8,128)(2,1)}) %all-gather.20.cloned.1.call-update) | async-done | bytes 2097168 | tf_op jit(solution)/shard_map/all_gather | solution.py:18
  220.2 3.8 fusion.23
  223.9 45.7 %all-gather.36.cloned.1.call-done = bf16[1,1,1024,1024]{3,2,1,0:T(8,128)(2,1)} async-done(((bf16[1,1,128,1024]{3,2,1,0:T(8,128)(2,1)}), bf16[1,1,1024,1024]{3,2,1,0:T(8,128)(2,1)}) %all-gather.36.cloned.1.call-update) | async-done | bytes 2097168 | tf_op jit(solution)/shard_map/all_gather | solution.py:32
  269.7 51.5 %all-gather.22.cloned.1.call-done = bf16[1024,1024]{0,1:T(8,128)(2,1)} async-done(((bf16[128,1024]{0,1:T(8,128)(2,1)}), bf16[1024,1024]{0,1:T(8,128)(2,1)}) %all-gather.22.cloned.1.call-update) | async-done | bytes 2097168 | tf_op jit(solution)/shard_map/all_gather | solution.py:18
  324.9 45.7 %all-gather.38.cloned.1.call-done = bf16[1,1,1024,1024]{3,2,1,0:T(8,128)(2,1)} async-done(((bf16[1,1,128,1024]{3,2,1,0:T(8,128)(2,1)}), bf16[1,1,1024,1024]{3,2,1,0:T(8,128)(2,1)}) %all-gather.38.cloned.1.call-update) | async-done | bytes 2097168 | tf_op jit(solution)/shard_map/all_gather | solution.py:32
  370.6 51.6 %all-gather.24.cloned.1.call-done = bf16[1024,1024]{0,1:T(8,128)(2,1)} async-done(((bf16[128,1024]{0,1:T(8,128)(2,1)}), bf16[1024,1024]{0,1:T(8,128)(2,1)}) %all-gather.24.cloned.1.call-update) | async-done | bytes 2097168 | tf_op jit(solution)/shard_map/all_gather | solution.py:18
  422.3 3.8 fusion.35
  426.0 45.9 %all-gather.40.cloned.1.call-done = bf16[1,1,1024,1024]{3,2,1,0:T(8,128)(2,1)} async-done(((bf16[1,1,128,1024]{3,2,1,0:T(8,128)(2,1)}), bf16[1,1,1024,1024]{3,2,1,0:T(8,128)(2,1)}) %all-gather.40.cloned.1.call-update) | async-done | bytes 2097168 | tf_op jit(solution)/shard_map/all_gather | solution.py:32
  471.9 51.6 %all-gather.26.cloned.1.call-done = bf16[1024,1024]{0,1:T(8,128)(2,1)} async-done(((bf16[128,1024]{0,1:T(8,128)(2,1)}), bf16[1024,1024]{0,1:T(8,128)(2,1)}) %all-gather.26.cloned.1.call-update) | async-done | bytes 2097168 | tf_op jit(solution)/shard_map/all_gather | solution.py:18
  523.6 3.8 fusion.41
  527.3 45.7 %all-gather.42.cloned.1.call-done = bf16[1,1,1024,1024]{3,2,1,0:T(8,128)(2,1)} async-done(((bf16[1,1,128,1024]{3,2,1,0:T(8,128)(2,1)}), bf16[1,1,1024,1024]{3,2,1,0:T(8,128)(2,1)}) %all-gather.42.cloned.1.call-update) | async-done | bytes 2097168 | tf_op jit(solution)/shard_map/all_gather | solution.py:32
  573.0 51.6 %all-gather.28.cloned.1.call-done = bf16[1024,1024]{0,1:T(8,128)(2,1)} async-done(((bf16[128,1024]{0,1:T(8,128)(2,1)}), bf16[1024,1024]{0,1:T(8,128)(2,1)}) %all-gather.28.cloned.1.call-update) | async-done | bytes 2097168 | tf_op jit(solution)/shard_map/all_gather | solution.py:18
  628.5 46.3 %all-gather.44.cloned.1.call-done = bf16[1,1,1024,1024]{3,2,1,0:T(8,128)(2,1)} async-done(((bf16[1,1,128,1024]{3,2,1,0:T(8,128)(2,1)}), bf16[1,1,1024,1024]{3,2,1,0:T(8,128)(2,1)}) %all-gather.44.cloned.1.call-update) | async-done | bytes 2097168 | tf_op jit(solution)/shard_map/all_gather | solution.py:32
  674.7 51.6 %all-gather.30.cloned.1.call-done = bf16[1024,1024]{0,1:T(8,128)(2,1)} async-done(((bf16[128,1024]{0,1:T(8,128)(2,1)}), bf16[1024,1024]{0,1:T(8,128)(2,1)}) %all-gather.30.cloned.1.call-update) | async-done | bytes 2097168 | tf_op jit(solution)/shard_map/all_gather | solution.py:18
  730.5 18.8 %all-reduce = (f32[6]{0:T(128)S(1)}, f32[6]{0:T(128)S(1)}) all-reduce(f32[6]{0:T(128)S(1)} %multiply_reduce_fusion.1, f32[6]{0:T(128)S(1)} %fusion.7), channel_id=1, replica_groups=mesh['dp'=8,'owner'=4] {'dp'}, use_global_device_ids=true, to_apply=%region_5.0 | all-reduce | flops 12 | bytes 96 | tf_op jit(solution)/shard_map/psum | solution.py:79
  753.2 4.0 copy.85
  760.9 25.6 %all-to-all-done.1 = bf16[6,128,1024]{1,0,2:T(8,128)(2,1)S(1)} async-done(((bf16[6,128,1024]{1,0,2:T(8,128)(2,1)}), bf16[6,128,1024]{1,0,2:T(8,128)(2,1)S(1)}, u32[]{:S(2)}, u32[]{:S(2)}) %all-to-all-start.1) | async-done | bytes 1572896 | tf_op jit(solution)/shard_map/all_to_all | solution.py:86
  793.9 6.4 fusion
  824.7 52.0 %all-gather.32.cloned.1.call-done = bf16[10,1024,256]{2,1,0:T(8,128)(2,1)} async-done(((bf16[10,128,256]{2,1,0:T(8,128)(2,1)}), bf16[10,1024,256]{2,1,0:T(8,128)(2,1)}) %all-gather.32.cloned.1.call-update) | async-done | bytes 5242896 | tf_op jit(solution)/shard_map/all_gather | solution.py:88
  876.7 5.2 copy.109
  (114 shorter events, 74.9 us)
Async XLA Ops:
  7.2 110.1 %reduce-scatter.2.cloned.1.call-start = ((), (), s32[]{:S(2)}) async-start(), calls=%async_computation.3 | async-start | bytes 5898240 | tf_op jit(solution)/shard_map/reduce_scatter | solution.py:55
  7.9 2.0 copy-start.19
  7.9 163.1 %all-gather.34.cloned.1.call-start = ((), (), s32[]{:S(2)}) async-start(), calls=%async_computation.11 | async-start | bytes 2359296 | tf_op jit(solution)/shard_map/all_gather | solution.py:32
  9.8 210.4 %all-gather.20.cloned.1.call-start = ((), (), s32[]{:S(2)}) async-start(), calls=%async_computation.4 | async-start | bytes 2359296 | tf_op jit(solution)/shard_map/all_gather | solution.py:18
  144.2 125.4 %all-gather.36.cloned.1.call-start = ((), (), s32[]{:S(2)}) async-start(), calls=%async_computation.12 | async-start | bytes 2359296 | tf_op jit(solution)/shard_map/all_gather | solution.py:32
  144.8 176.4 %all-gather.22.cloned.1.call-start = ((), (), s32[]{:S(2)}) async-start(), calls=%async_computation.5 | async-start | bytes 2359296 | tf_op jit(solution)/shard_map/all_gather | solution.py:18
  145.7 224.9 %all-gather.38.cloned.1.call-start = ((), (), s32[]{:S(2)}) async-start(), calls=%async_computation.13 | async-start | bytes 2359296 | tf_op jit(solution)/shard_map/all_gather | solution.py:32
  146.3 276.0 %all-gather.24.cloned.1.call-start = ((), (), s32[]{:S(2)}) async-start(), calls=%async_computation.6 | async-start | bytes 2359296 | tf_op jit(solution)/shard_map/all_gather | solution.py:18
  147.2 324.7 %all-gather.40.cloned.1.call-start = ((), (), s32[]{:S(2)}) async-start(), calls=%async_computation.14 | async-start | bytes 2359296 | tf_op jit(solution)/shard_map/all_gather | solution.py:32
  147.9 375.6 %all-gather.26.cloned.1.call-start = ((), (), s32[]{:S(2)}) async-start(), calls=%async_computation.7 | async-start | bytes 2359296 | tf_op jit(solution)/shard_map/all_gather | solution.py:18
  148.9 424.2 %all-gather.42.cloned.1.call-start = ((), (), s32[]{:S(2)}) async-start(), calls=%async_computation.15 | async-start | bytes 2359296 | tf_op jit(solution)/shard_map/all_gather | solution.py:32
  149.4 475.2 %all-gather.28.cloned.1.call-start = ((), (), s32[]{:S(2)}) async-start(), calls=%async_computation.8 | async-start | bytes 2359296 | tf_op jit(solution)/shard_map/all_gather | solution.py:18
  150.4 524.4 %all-gather.44.cloned.1.call-start = ((), (), s32[]{:S(2)}) async-start(), calls=%async_computation.16 | async-start | bytes 2359296 | tf_op jit(solution)/shard_map/all_gather | solution.py:32
  150.9 575.5 %all-gather.30.cloned.1.call-start = ((), (), s32[]{:S(2)}) async-start(), calls=%async_computation.9 | async-start | bytes 2359296 | tf_op jit(solution)/shard_map/all_gather | solution.py:18
  154.4 11.7 %copy-start = (f32[1,6,128,1024]{2,3,1,0:T(8,128)}, f32[1,6,128,1024]{2,3,1,0:T(8,128)S(1)}, u32[]{:S(2)}) copy-start(f32[1,6,128,1024]{2,3,1,0:T(8,128)S(1)} %copy.81) | copy-start | bytes 9437188
  749.3 2.2 copy-start.9
  757.2 29.3 %all-to-all-start.1 = ((bf16[6,128,1024]{1,0,2:T(8,128)(2,1)}), bf16[6,128,1024]{1,0,2:T(8,128)(2,1)S(1)}, u32[]{:S(2)}, u32[]{:S(2)}) async-start(bf16[6,128,1024]{1,0,2:T(8,128)(2,1)} %copy.85), calls=%async_computation.2 | async-start | bytes 4194304 | tf_op jit(solution)/shard_map/all_to_all | solution.py:86
  760.8 115.9 %all-gather.32.cloned.1.call-start = ((), (), s32[]{:S(2)}) async-start(), calls=%async_computation.10 | async-start | bytes 5898240 | tf_op jit(solution)/shard_map/all_gather | solution.py:88
  788.8 5.1 copy-start.1
  803.9 3.7 copy-start.2
  807.6 2.4 copy-start.4
  810.1 1.8 copy-start.6
  817.4 1.9 copy-start.10
  819.3 2.7 copy-start.11
  (11 other events, 14.6 us)
Sparse Core Ops, SparseCore 0:
  11.6 105.6 reduce-scatter.1
  119.4 49.0 all-gather.33
  170.6 49.5 all-gather.19
  222.1 47.4 all-gather.35
  271.5 49.5 all-gather.21
  323.1 47.4 all-gather.37
  372.7 49.5 all-gather.23
  424.4 47.4 all-gather.39
  474.0 49.5 all-gather.25
  525.5 47.4 all-gather.41
  575.1 49.5 all-gather.27
  627.2 47.4 all-gather.43
  676.8 49.5 all-gather.29
  794.1 82.5 all-gather.31
where the time goes:
time: 889 us; the launch traced here: 888 us
  waiting for transfers between devices  725 us (82%)
  local copies, waits for them, and re-layouts  44.6 us (5%)
  blocking collectives  41.4 us (5%)
  matrix products  32.2 us (4%)
  other arithmetic  26.6 us (3%)
  between operations  14.2 us (2%)
    all_gather x6, waiting for transfers between devices, precondition(): piece = lax.all_gather(rounded, 'dp', axis=0, tiled=True)  307 us
    all_gather x6, waiting for transfers between devices, precondition(): lax.all_gather(right_rows, 'dp', axis=0, tiled=True)  229 us
    reduce_scatter x1, waiting for transfers between devices, per_device(): lax.psum_scatter(grads[0].astype(jnp.float32).astype(jnp.bfloat16), 'dp',...  107 us
    all_gather x1, waiting for transfers between devices, per_device(): new_weights = lax.all_gather(picked, 'dp', axis=1, tiled=True)  52 us
    all_to_all x1, waiting for transfers between devices, per_device(): lax.all_to_all(finished, 'owner', split_axis=2, concat_axis=0, tiled=True)  25.6 us
    unnamed x45, local copies, waits for them, and re-layouts  25.1 us
    all_to_all x1, blocking collectives, per_device(): lax.all_to_all(outgoing.astype(jnp.bfloat16), 'owner', split_axis=0, conc...  22.6 us
    dot_general x6, matrix products, precondition(): jnp.dot(half, lax.all_gather(right_rows, 'dp', axis=0, tiled=True), prefe...  22.6 us
  transfers between devices with their start and end apart: 15, of which 14 were waited for; matrix products, arithmetic and copies ran while one was open for 8% of the time, Pallas kernels for 0%

commit v1 on v0

v1 whole, which is shorter than its diff:
```python
import jax
import jax.numpy as jnp
from jax import lax
from jax.sharding import Mesh, PartitionSpec as P

CORES = 2
GRID = ("y", "core")


def slot_table(owner_of):
    count = owner_of.shape[0]
    here = lax.broadcasted_iota(jnp.int32, (count, count), 0)
    prior = lax.broadcasted_iota(jnp.int32, (count, count), 1)
    same = (owner_of[:, None] == owner_of[None, :]) & (prior < here)
    return jnp.sum(same.astype(jnp.int32), axis=1)


def sum_rows(grads):
    return lax.psum_scatter(grads, "dp", scatter_dimension=1, tiled=True)


def gather_rows(part):
    return lax.all_gather(part, ("dp", "core"), axis=1, tiled=True)


def dot(a, b, dims):
    return lax.dot_general(a, b, (dims, ((0,), (0,))), preferred_element_type=jnp.float32)


def per_device(
    grads,
    owner_of,
    left_stats,
    right_stats,
    left_root,
    right_root,
    weights,
    first_moment,
    second_moment,
):
    planes = lax.axis_size("y")
    y = lax.axis_index("y")
    core = lax.axis_index("core")
    me = y * CORES + core
    slots, rows, width = left_stats.shape[1:]
    count = owner_of.shape[0]
    per_plane = -(-count // planes)
    padded = per_plane * planes
    part = rows // CORES
    slot_of = slot_table(owner_of)

    mine = owner_of == me
    slot_at = lax.broadcasted_iota(jnp.int32, (slots, count), 0)
    holds = mine[None, :] & (slot_of[None, :] == slot_at)
    has = jnp.any(holds, axis=1)
    block_of = jnp.argmax(holds, axis=1).astype(jnp.int32)

    def by_block(array):
        picked = jnp.where(mine[:, None, None], jnp.take(array[0], slot_of, axis=0), 0)
        return jnp.pad(picked, ((0, padded - count), (0, 0), (0, 0)))

    def to_plane(arrays):
        picked = jnp.stack([by_block(array) for array in arrays])
        kinds = len(arrays)
        picked = picked.reshape(kinds, planes, per_plane, CORES, part, width)
        picked = picked.transpose(1, 3, 0, 2, 4, 5).reshape(-1, kinds * per_plane, part, width)
        out = lax.psum_scatter(picked, GRID, scatter_dimension=0, tiled=True)
        return out.reshape(kinds, per_plane, part, width)

    rroot, lroot, weight = to_plane((right_root, left_root, weights))
    rroot_all = gather_rows(rroot)

    reduced = sum_rows(grads[0])
    summed = lax.all_gather(reduced, GRID, axis=2, tiled=True)
    wide = jnp.pad(summed, ((0, padded - count), (0, 0), (0, 0)))
    own = lax.dynamic_slice(wide, (y * per_plane, core * part, 0), (per_plane, part, width))
    full = gather_rows(own)

    first_row = lax.axis_index("dp") * rows + core * part
    own_cols = lax.dynamic_slice_in_dim(full, first_row, part, 2)
    half = dot(lroot, full, ((2,), (1,))).astype(jnp.bfloat16)
    left_inc = dot(own, full, ((2,), (2,))).astype(jnp.bfloat16)
    right_inc = dot(own_cols, full, ((1,), (1,))).astype(jnp.bfloat16)
    incs = lax.all_gather(jnp.stack([left_inc, right_inc]), GRID)
    incs = incs.reshape(planes, CORES, 2, per_plane, part, width)
    incs = incs.transpose(2, 0, 3, 1, 4, 5).reshape(2, padded, rows, width)

    def to_slots(array):
        return jnp.where(has[:, None, None], jnp.take(array, block_of, axis=0), 0).astype(jnp.float32)

    owned = to_slots(summed)
    new_left = 0.95 * left_stats[0] + to_slots(incs[0])
    new_right = 0.95 * right_stats[0] + to_slots(incs[1])
    new_first = 0.9 * first_moment[0] + 0.1 * owned
    new_second = 0.999 * second_moment[0] + 0.001 * owned * owned
    adam = new_first / (jnp.sqrt(new_second) + 1e-08)
    adam_sq = jnp.sum(adam * adam, axis=(1, 2))
    adam_part = jnp.sum(jnp.where(holds, adam_sq[:, None], 0.0), axis=0)

    direction = dot(half, rroot_all, ((2,), (1,)))
    dir_sq = jnp.sum(direction * direction, axis=(1, 2))
    dir_part = lax.dynamic_update_slice(jnp.zeros((padded,), jnp.float32), dir_sq, (y * per_plane,))
    totals = lax.psum(
        jnp.concatenate([jnp.pad(adam_part, (0, padded - count)), dir_part]), ("dp",) + GRID
    )
    graft = jnp.sqrt(totals[:padded]) / jnp.sqrt(totals[padded:] + 1e-12)
    graft = lax.dynamic_slice(graft, (y * per_plane,), (per_plane,))
    moved = weight.astype(jnp.float32) - 0.1 * graft[:, None, None] * direction
    updated = moved * lax.rsqrt(jnp.mean(moved * moved, axis=-1, keepdims=True) + 1e-06)
    finished = updated.astype(jnp.bfloat16).reshape(per_plane, part, planes * CORES, -1)
    by_cols = lax.all_to_all(finished, GRID, split_axis=2, concat_axis=0, tiled=False)
    by_cols = by_cols.reshape(planes, CORES, per_plane, part, -1)
    by_cols = by_cols.transpose(0, 2, 1, 3, 4).reshape(padded, rows, -1)[:count]
    new_weights = lax.all_gather(by_cols, "dp", axis=1, tiled=True)
    return (new_left[None], new_right[None], new_first[None], new_second[None], new_weights)


def solution(mesh):
    dp, owners = mesh.shape["dp"], mesh.shape["owner"]
    grid = Mesh(mesh.devices.reshape(dp, owners // CORES, CORES), ("dp",) + GRID)
    rows = P(GRID, None, "dp", None)
    return jax.shard_map(
        per_device,
        mesh=grid,
        in_specs=(P("dp", None, None, GRID), P()) + (rows,) * 7,
        out_specs=(rows,) * 4 + (P(None, None, GRID),),
        check_vma=False,
    )
```

time: 889 us -> 619 us (0.70)
  waiting for transfers between devices: 725 us -> 467 us
  blocking collectives: 41.4 us -> 52.9 us
  matrix products: 32.2 us -> 21.6 us
    all_gather x13 -> x5, waiting for transfers between devices: 589 us -> 287 us  [the longest x2 162 us: gather_rows(): return lax.all_gather(part, ('dp', 'core'), axis=1, tiled=True)]
    reduce_scatter x1 -> x2, waiting for transfers between devices: 107 us -> 179 us  [the longest x1 109 us: sum_rows(): return lax.psum_scatter(grads, 'dp', scatter_dimension=1, tiled=True)]
    all_to_all x1 -> x0, waiting for transfers between devices: 25.6 us -> none  [per_device(): lax.all_to_all(finished, 'owner', split_axis=2, concat_axis=0, tiled=True)]
    psum x1, blocking collectives: 18.8 us -> 39.3 us  [per_device(): lax.psum(jnp.concatenate([jnp.pad(adam_part, (0, padded - count)), dir_pa...]
    unnamed x45 -> x15, local copies, waits for them, and re-layouts: 25.1 us -> 5.8 us
    gather x1 -> x6, local copies, waits for them, and re-layouts: 3.02 us -> 16.6 us  [the longest x3 9.56 us: to_slots(): jnp.take(array, block_of, axis=0)]
    add x3 -> x0, other arithmetic: 11.8 us -> none  [the longest x1 6.44 us: per_device(): new_second = 0.999 * second_moment[0] + 0.001 * owned * owned]
    dot_general x19 -> x3, matrix products: 32.2 us -> 21.6 us  [dot(): lax.dot_general(a, b, (dims, ((0,), (0,))), preferred_element_type=jnp.fl...]
  transfers between devices with their start and end apart: 15 -> 7, of which waited for: 14 -> 7; matrix products, arithmetic and copies ran while one was open for 8% -> 8% of each run, Pallas kernels for 0% -> 0%
where the time goes in v1:
time: 619 us
  waiting for transfers between devices  467 us (75%)
  blocking collectives  52.9 us (9%)
  local copies, waits for them, and re-layouts  42.3 us (7%)
  matrix products  21.6 us (3%)
  other arithmetic  20.3 us (3%)
  between operations  14.3 us (2%)
    all_gather x2, waiting for transfers between devices, gather_rows(): return lax.all_gather(part, ('dp', 'core'), axis=1, tiled=True)  162 us
    reduce_scatter x1, waiting for transfers between devices, sum_rows(): return lax.psum_scatter(grads, 'dp', scatter_dimension=1, tiled=True)  109 us
    all_gather x1, waiting for transfers between devices, per_device(): new_weights = lax.all_gather(by_cols, 'dp', axis=1, tiled=True)  85.5 us
    reduce_scatter x1, waiting for transfers between devices, to_plane(): out = lax.psum_scatter(picked, GRID, scatter_dimension=0, tiled=True)  69.5 us
    psum x1, blocking collectives, per_device(): lax.psum(jnp.concatenate([jnp.pad(adam_part, (0, padded - count)), dir_pa...  39.3 us
    all_gather x1, waiting for transfers between devices, per_device(): incs = lax.all_gather(jnp.stack([left_inc, right_inc]), GRID)  29.1 us
    dot_general x3, matrix products, dot(): lax.dot_general(a, b, (dims, ((0,), (0,))), preferred_element_type=jnp.fl...  21.6 us
    all_to_all x1, blocking collectives, per_device(): lax.all_to_all(finished, GRID, split_axis=2, concat_axis=0, tiled=False)  13.6 us
  transfers between devices with their start and end apart: 7, of which 7 were waited for; matrix products, arithmetic and copies ran while one was open for 8% of the time, Pallas kernels for 0%

profile of v1, /device:TPU:0, one launch (start us, length us, event | category | flops | bytes accessed | tf_op | source)
XLA Modules:
  0.0 618.8 jit_solution(9820645704782249723)
XLA Ops:
  8.0 109.4 %reduce-scatter.3.cloned.1.call-done = bf16[10,128,256]{2,1,0:T(8,128)(2,1)} async-done(((bf16[10,1024,256]{2,1,0:T(8,128)(2,1)}), bf16[10,128,256]{2,1,0:T(8,128)(2,1)}) %reduce-scatter.3.cloned.1.call-update) | async-done | bytes 655376 | tf_op jit(solution)/shard_map/reduce_scatter | solution.py:19
  117.6 2.4 gather_fusion.4
  120.0 2.4 gather_fusion.5
  122.3 2.4 gather_fusion.3
  124.7 4.3 select_select_fusion.2
  130.0 4.1 copy.48
  134.2 10.4 %all-gather.8.cloned.1.call-done = bf16[10,128,1024]{2,1,0:T(8,128)(2,1)} async-done(((bf16[10,128,256]{2,1,0:T(8,128)(2,1)}), bf16[10,128,1024]{2,1,0:T(8,128)(2,1)}) %all-gather.8.cloned.1.call-update) | async-done | bytes 2621456 | tf_op jit(solution)/shard_map/all_gather | solution.py:74
  146.6 69.5 %reduce-scatter.5.cloned.1.call-done = bf16[1,15,64,1024]{3,2,1,0:T(8,128)(2,1)} async-done(((bf16[4,15,64,1024]{3,2,1,0:T(8,128)(2,1)}), bf16[1,15,64,1024]{3,2,1,0:T(8,128)(2,1)}) %reduce-scatter.5.cloned.1.call-update) | async-done | bytes 1966096 | tf_op jit(solution)/shard_map/reduce_scatter | solution.py:67
  218.2 88.7 %all-gather.10.cloned.1.call-done = bf16[5,1024,1024]{2,1,0:T(8,128)(2,1)} async-done(((bf16[5,64,1024]{2,1,0:T(8,128)(2,1)}), bf16[5,1024,1024]{2,1,0:T(8,128)(2,1)}) %all-gather.10.cloned.1.call-update) | async-done | bytes 10485776 | tf_op jit(solution)/shard_map/all_gather | solution.py:23
  307.0 6.9 %fusion.10 = bf16[1,5,64,1024]{3,2,1,0:T(8,128)(2,1)S(1)} fusion(bf16[5,1024,1024]{2,1,0:T(8,128)(2,1)} %all-gather.10.cloned.1.call-done, s32[]{:T(128)S(6)} %select_n.55), kind=kOutput, calls=%fused_computation.36 | convolution fusion | flops 671416320 | bytes 12451844 | tf_op jit(solution)/shard_map/dot_general | solution.py:27
  314.3 3.3 fusion.9
  319.9 2.4 gather_fusion.2
  322.2 73.7 %all-gather.16.cloned.1.call-done = bf16[1,5,1024,1024]{3,2,1,0:T(8,128)(2,1)} async-done(((bf16[1,5,64,1024]{3,2,1,0:T(8,128)(2,1)}), bf16[1,5,1024,1024]{3,2,1,0:T(8,128)(2,1)}) %all-gather.16.cloned.1.call-update) | async-done | bytes 10485776 | tf_op jit(solution)/shard_map/all_gather | solution.py:23
  395.9 11.4 %multiply_reduce_fusion.2 = (f32[5]{0:T(128)S(1)}, f32[5,64,1024]{2,1,0:T(8,128)S(1)}) fusion(bf16[1,5,1024,1024]{3,2,1,0:T(8,128)(2,1)} %all-gather.16.cloned.1.call-done, bf16[5,1024,1024]{2,1,0:T(8,128)(2,1)} %all-gather.10.cloned.1.call-done, bf16[1,15,64,1024]{3,2,1,0:T(8,128)(2,1)} %reduce-scatter.5.cloned.1.call-done), kind=kOutput, calls=%fused_computation.33 | convolution fusion | flops 1343160320 | bytes 22937620 | tf_op jit(solution)/shard_map/dot_general | solution.py:27
  407.5 29.1 %all-gather.14.cloned.1.call-done = bf16[8,5,64,1024]{3,2,1,0:T(8,128)(2,1)} async-done(((bf16[2,5,64,1024]{3,2,1,0:T(8,128)(2,1)}), bf16[8,5,64,1024]{3,2,1,0:T(8,128)(2,1)}) %all-gather.14.cloned.1.call-update) | async-done | bytes 5242896 | tf_op jit(solution)/shard_map/all_gather | solution.py:84
  436.6 4.8 fusion.17
  443.2 3.6 gather_fusion
  446.8 3.6 copy.41
  450.3 3.6 gather_fusion.1
  453.9 9.7 %multiply_reduce_fusion = (f32[6]{0:T(128)S(1)}, f32[1,6,128,1024]{3,2,1,0:T(8,128)}, f32[1,6,128,1024]{3,2,1,0:T(8,128)}, f32[1,6,128,1024]{3,2,1,0:T(8,128)}, f32[1,6,128,1024]{3,2,1,0:T(8,128)}) fusion(f32[1,6,128,1024]{3,2,1,0:T(8,128)} %param.20, f32[1,6,128,1024]{3,2,1,0:T(8,128)} %param.21, bf16[6,128,1024]{2,1,0:T(8,128)(2,1)S(1)} %gather_fusion.2, ...), kind=kLoop, calls=%fused_computation.17 | loop fusion | flops 18874362 | bytes 29884452 | tf_op jit(solution)/shard_map/reduce_sum | solution.py:97
  463.8 39.3 %psum.7 = f32[20]{0:T(128)S(1)} all-reduce(f32[20]{0:T(128)S(1)} %pad_maximum_fusion.2), channel_id=1, replica_groups=mesh['dp'=8,'y'=2,'core'=2] {'dp','y','core'}, use_global_device_ids=true, to_apply=%region_8.11 | all-reduce | flops 20 | bytes 160 | tf_op jit(solution)/shard_map/psum | solution.py:103
  506.6 13.6 %all_to_all.15 = bf16[1,5,64,4,256]{4,2,1,0,3:T(8,128)(2,1)S(1)} all-to-all(bf16[1,5,64,4,256]{4,2,1,0,3:T(8,128)(2,1)S(1)} %copy.45), channel_id=1, replica_groups=mesh['dp'=8,'y'=2,'core'=2] {'y','core'}, dimensions={3} | all-to-all | bytes 1310720 | tf_op jit(solution)/shard_map/all_to_all | solution.py:111
  521.1 85.5 %all-gather.12.cloned.1.call-done = bf16[10,1024,256]{2,1,0:T(8,128)(2,1)} async-done(((bf16[10,128,256]{2,1,0:T(8,128)(2,1)}), bf16[10,1024,256]{2,1,0:T(8,128)(2,1)}) %all-gather.12.cloned.1.call-update) | async-done | bytes 5242896 | tf_op jit(solution)/shard_map/all_gather | solution.py:114
  606.6 5.3 copy.51
  (55 shorter events, 15.3 us)
Async XLA Ops:
  7.2 110.4 %copy-start = (bf16[1,6,128,1024]{3,2,1,0:T(8,128)(2,1)S(1)}, bf16[1,6,128,1024]{3,2,1,0:T(8,128)(2,1)}, u32[]{:S(2)}) copy-start(bf16[1,6,128,1024]{3,2,1,0:T(8,128)(2,1)} %param.17) | copy-start | bytes 4718596
  7.2 110.1 %reduce-scatter.3.cloned.1.call-start = ((), (), s32[]{:S(2)}) async-start(), calls=%async_computation.3 | async-start | bytes 5898240 | tf_op jit(solution)/shard_map/reduce_scatter | solution.py:19
  7.2 110.2 %copy-start.6 = (s32[10]{0:T(128)S(1)}, s32[10]{0:T(128)}, u32[]{:S(2)}) copy-start(s32[10]{0:T(128)} %param.14) | copy-start | bytes 124
  7.9 136.6 %all-gather.8.cloned.1.call-start = ((), (), s32[]{:S(2)}) async-start(), calls=%async_computation.4 | async-start | bytes 3276800 | tf_op jit(solution)/shard_map/all_gather | solution.py:74
  117.3 98.8 %reduce-scatter.5.cloned.1.call-start = ((), (), s32[]{:S(2)}) async-start(), calls=%async_computation.6 | async-start | bytes 9830400 | tf_op jit(solution)/shard_map/reduce_scatter | solution.py:67
  117.6 2.4 copy-start.4
  120.0 2.4 copy-start.5
  134.1 172.8 %all-gather.10.cloned.1.call-start = ((), (), s32[]{:S(2)}) async-start(), calls=%async_computation.5 | async-start | bytes 11141120 | tf_op jit(solution)/shard_map/all_gather | solution.py:23
  146.6 249.3 %all-gather.16.cloned.1.call-start = ((), (), s32[]{:S(2)}) async-start(), calls=%async_computation.9 | async-start | bytes 11141120 | tf_op jit(solution)/shard_map/all_gather | solution.py:23
  218.2 218.5 %all-gather.14.cloned.1.call-start = ((), (), s32[]{:S(2)}) async-start(), calls=%async_computation.8 | async-start | bytes 6553600 | tf_op jit(solution)/shard_map/all_gather | solution.py:84
  218.2 95.6 %copy-start.3 = (bf16[5,64,1024]{2,1,0:T(8,128)(2,1)S(1)}, bf16[5,64,1024]{2,1,0:T(8,128)(2,1)}, u32[]{:S(2)}) copy-start(bf16[5,64,1024]{2,1,0:T(8,128)(2,1)} %constant_dynamic-slice_fusion) | copy-start | bytes 1966084
  306.9 7.4 %copy-start.2 = (bf16[5,1024,1024]{2,1,0:T(8,128)(2,1)S(1)}, bf16[5,1024,1024]{2,1,0:T(8,128)(2,1)}, u32[]{:S(2)}) copy-start(bf16[5,1024,1024]{2,1,0:T(8,128)(2,1)} %all-gather.10.cloned.1.call-done) | copy-start | bytes 31457284
  318.8 287.8 %all-gather.12.cloned.1.call-start = ((), (), s32[]{:S(2)}) async-start(), calls=%async_computation.7 | async-start | bytes 5898240 | tf_op jit(solution)/shard_map/all_gather | solution.py:114
  606.6 5.3 copy-start.1
Sparse Core Ops, SparseCore 0:
  11.6 105.6 reduce-scatter.2
  118.9 25.6 all-gather.7
  147.1 68.9 reduce-scatter.4
  219.0 87.9 all-gather.9
  309.8 86.0 all-gather.15
  398.0 38.6 all-gather.13
  521.2 85.3 all-gather.11

commit v2 on v1

--- a/solution.py
+++ b/solution.py
@@ -1,7 +1,13 @@
+import functools
+
 import jax
 import jax.numpy as jnp
 from jax import lax
+from jax.experimental import pallas as pl
+from jax.experimental.pallas import tpu as pltpu
 from jax.sharding import Mesh, PartitionSpec as P
+
+MESH = pl.DeviceIdType.MESH
 
 CORES = 2
 GRID = ("y", "core")
@@ -15,8 +21,179 @@
     return jnp.sum(same.astype(jnp.int32), axis=1)
 
 
+def grid_of(n):
+    width = 1
+    while 2 * (2 * width) ** 2 <= n:
+        width *= 2
+    return n // width, width
+
+
+def position_of(index, n):
+    depth, width = grid_of(n)
+    z, x = index // width, index % width
+    row = depth - 1 - z
+    odd = row % 2
+    along = (1 - odd) * (x - 1) + odd * (width - 1 - x)
+    back = (x + width - 1) // width
+    return (1 - back) * z + back * (depth + row * (width - 1) + along)
+
+
+def index_at(position, n):
+    depth, width = grid_of(n)
+    back = (position // depth + width - 1) // width
+    rest = position - depth + (1 - back) * n
+    row, along = rest // (width - 1), rest % (width - 1)
+    odd = row % 2
+    x = (1 - odd) * (1 + along) + odd * (width - 1 - along)
+    return (1 - back) * position * width + back * ((depth - 1 - row) * width + x)
+
+
+def ring(n):
+    way = 1 - 2 * lax.axis_index("core")
+    place = position_of(lax.axis_index("dp"), n)
+    return place, way, index_at((place + way + n) % n, n), index_at((place - way + n) % n, n)
+
+
+def sum_kernel(n, rows, g_ref, out_ref, held, send_sem, recv_sem):
+    place, way, after, before = ring(n)
+    half = g_ref.shape[0] // 2
+    barrier = pltpu.get_barrier_semaphore()
+    pl.semaphore_signal(barrier, inc=1, device_id={"dp": before}, device_id_type=MESH)
+    pl.semaphore_wait(barrier, 1)
+
+    def terms(step, part):
+        row = index_at((place - way * (1 + step) + 2 * n) % n, n) * rows
+        return g_ref.at[pl.ds(part * half, half), pl.ds(pl.multiple_of(row, rows), rows), :]
+
+    def send(source, step, part):
+        return pltpu.make_async_remote_copy(
+            src_ref=source,
+            dst_ref=held.at[step, part],
+            send_sem=send_sem.at[step, part],
+            recv_sem=recv_sem.at[step, part],
+            device_id={"dp": after},
+            device_id_type=MESH,
+        )
+
+    def total(step, part):
+        came = held[step - 1, part].astype(jnp.float32)
+        return (came + terms(step, part)[...].astype(jnp.float32)).astype(jnp.bfloat16)
+
+    for part in range(2):
+        send(terms(0, part), 0, part).start()
+
+    @pl.loop(1, n - 1)
+    def _(step):
+        for part in range(2):
+            send(held.at[step - 1, part], step - 1, part).wait_recv()
+            held[step - 1, part] = total(step, part)
+            send(held.at[step - 1, part], step, part).start()
+
+    for part in range(2):
+        send(held.at[n - 2, part], n - 2, part).wait_recv()
+        out_ref[pl.ds(part * half, half)] = total(n - 1, part)
+
+    @pl.loop(0, n - 1)
+    def _(step):
+        for part in range(2):
+            send(held.at[step, part], step, part).wait_send()
+
+
 def sum_rows(grads):
-    return lax.psum_scatter(grads, "dp", scatter_dimension=1, tiled=True)
+    n = lax.axis_size("dp")
+    count, height, width = grads.shape
+    rows = height // n
+    return pl.pallas_call(
+        functools.partial(sum_kernel, n, rows),
+        out_shape=jax.ShapeDtypeStruct((count, rows, width), grads.dtype),
+        in_specs=[pl.BlockSpec(memory_space=pltpu.VMEM)],
+        out_specs=pl.BlockSpec(memory_space=pltpu.VMEM),
+        scratch_shapes=[
+            pltpu.VMEM((n - 1, 2, count // 2, rows, width), grads.dtype),
+            pltpu.SemaphoreType.DMA((n - 1, 2)),
+            pltpu.SemaphoreType.DMA((n - 1, 2)),
+        ],
+        compiler_params=pltpu.CompilerParams(
+            collective_id=0, has_side_effects=True, vmem_limit_bytes=24 * 2**20
+        ),
+        cost_estimate=pl.CostEstimate(flops=0, bytes_accessed=200_000_000, transcendentals=0),
+        name="sum_ring",
+    )(grads)
+
+
+def gather_kernel(n, shared, x_ref, out_ref, local_sem, send_sem, recv_sem, *pair_sems):
+    place, way, after, before = ring(n)
+    rows = x_ref.shape[1]
+    core = lax.axis_index("core")
+    other = {"core": 1 - core}
+    barrier = pltpu.get_barrier_semaphore()
+    pl.semaphore_signal(barrier, inc=1, device_id={"dp": before}, device_id_type=MESH)
+    if shared:
+        pl.semaphore_signal(barrier, inc=1, device_id=other, device_id_type=MESH)
+    pl.semaphore_wait(barrier, 2 if shared else 1)
+
+    def spot(step):
+        index = index_at((place - way * step + 2 * n) % n, n)
+        first = (index * CORES + core) * rows if shared else index * rows
+        return out_ref.at[:, pl.ds(pl.multiple_of(first, rows), rows), :]
+
+    def copy(step, sems, target):
+        return pltpu.make_async_remote_copy(
+            src_ref=spot(step),
+            dst_ref=spot(step),
+            send_sem=sems[0].at[step],
+            recv_sem=sems[1].at[step],
+            device_id=target,
+            device_id_type=MESH,
+        )
+
+    def onward(step):
+        return copy(step, (send_sem, recv_sem), {"dp": after})
+
+    own = pltpu.make_async_copy(x_ref, spot(0), local_sem)
+    own.start()
+    own.wait()
+    onward(0).start()
+    if shared:
+        copy(0, pair_sems, other).start()
+
+    @pl.loop(1, n)
+    def _(step):
+        onward(step - 1).wait_recv()
+
+        @pl.when(step < n - 1)
+        def _():
+            onward(step).start()
+
+        if shared:
+            copy(step, pair_sems, other).start()
+
+    @pl.loop(0, n)
+    def _(step):
+        @pl.when(step < n - 1)
+        def _():
+            onward(step).wait_send()
+
+        if shared:
+            copy(step, pair_sems, other).wait()
+
+
+def gather_ring(part, shared, number):
+    n = lax.axis_size("dp")
+    count, rows, width = part.shape
+    height = n * rows * (CORES if shared else 1)
+    return pl.pallas_call(
+        functools.partial(gather_kernel, n, shared),
+        out_shape=jax.ShapeDtypeStruct((count, height, width), part.dtype),
+        in_specs=[pl.BlockSpec(memory_space=pl.ANY)],
+        out_specs=pl.BlockSpec(memory_space=pl.ANY),
+        scratch_shapes=[pltpu.SemaphoreType.DMA]
+        + [pltpu.SemaphoreType.DMA((n - 1,))] * 2
+        + ([pltpu.SemaphoreType.DMA((n,))] * 2 if shared else []),
+        compiler_params=pltpu.CompilerParams(collective_id=number, has_side_effects=True),
+        cost_estimate=pl.CostEstimate(flops=0, bytes_accessed=200_000_000, transcendentals=0),
+        name="gather_ring_%d" % number,
+    )(part)
 
 
 def gather_rows(part):
@@ -56,7 +233,10 @@
     block_of = jnp.argmax(holds, axis=1).astype(jnp.int32)
 
     def by_block(array):
-        picked = jnp.where(mine[:, None, None], jnp.take(array[0], slot_of, axis=0), 0)
+        picked = jnp.stack([
+            jnp.where(mine[m], lax.dynamic_index_in_dim(array[0], slot_of[m], 0, False), 0)
+            for m in range(count)
+        ])
         return jnp.pad(picked, ((0, padded - count), (0, 0), (0, 0)))
 
     def to_plane(arrays):
@@ -74,7 +254,7 @@
     summed = lax.all_gather(reduced, GRID, axis=2, tiled=True)
     wide = jnp.pad(summed, ((0, padded - count), (0, 0), (0, 0)))
     own = lax.dynamic_slice(wide, (y * per_plane, core * part, 0), (per_plane, part, width))
-    full = gather_rows(own)
+    full = gather_ring(own, True, 1)
 
     first_row = lax.axis_index("dp") * rows + core * part
     own_cols = lax.dynamic_slice_in_dim(full, first_row, part, 2)
@@ -86,7 +266,10 @@
     incs = incs.transpose(2, 0, 3, 1, 4, 5).reshape(2, padded, rows, width)
 
     def to_slots(array):
-        return jnp.where(has[:, None, None], jnp.take(array, block_of, axis=0), 0).astype(jnp.float32)
+        return jnp.stack([
+            jnp.where(has[k], lax.dynamic_index_in_dim(array, block_of[k], 0, False), 0)
+            for k in range(slots)
+        ]).astype(jnp.float32)
 
     owned = to_slots(summed)
     new_left = 0.95 * left_stats[0] + to_slots(incs[0])
@@ -111,7 +294,7 @@
     by_cols = lax.all_to_all(finished, GRID, split_axis=2, concat_axis=0, tiled=False)
     by_cols = by_cols.reshape(planes, CORES, per_plane, part, -1)
     by_cols = by_cols.transpose(0, 2, 1, 3, 4).reshape(padded, rows, -1)[:count]
-    new_weights = lax.all_gather(by_cols, "dp", axis=1, tiled=True)
+    new_weights = gather_ring(by_cols, False, 2)
     return (new_left[None], new_right[None], new_first[None], new_second[None], new_weights)
 
 

time: 619 us -> 545 us (0.88)
  waiting for transfers between devices: 467 us -> 81.2 us
  Pallas kernels: 0 us -> 241 us
  other arithmetic: 20.3 us -> 79.9 us
  between operations: 14.3 us -> 45.1 us
  blocking collectives: 52.9 us -> 38.6 us
  local copies, waits for them, and re-layouts: 42.3 us -> 31.6 us
    pallas_call x0 -> x3, Pallas kernels: none -> 241 us  [the longest x2 186 us: gather_ring(): pl.pallas_call(functools.partial(gather_kernel, n, shared), out_shape=jax...]
    reduce_scatter x1 -> x0, waiting for transfers between devices: 109 us -> none  [sum_rows(): return lax.psum_scatter(grads, 'dp', scatter_dimension=1, tiled=True)]
    all_gather x2 -> x1, waiting for transfers between devices: 162 us -> 67.3 us  [gather_rows(): return lax.all_gather(part, ('dp', 'core'), axis=1, tiled=True)]
    all_gather x1 -> x0, waiting for transfers between devices: 85.5 us -> none  [per_device(): new_weights = lax.all_gather(by_cols, 'dp', axis=1, tiled=True)]
    reduce_scatter x1, waiting for transfers between devices: 69.5 us -> 0.02 us  [to_plane(): out = lax.psum_scatter(picked, GRID, scatter_dimension=0, tiled=True)]
    unnamed x0 -> x45, other arithmetic: none -> 50.6 us
    all_gather x1, waiting for transfers between devices: 29.1 us -> 9.45 us  [per_device(): incs = lax.all_gather(jnp.stack([left_inc, right_inc]), GRID)]
    gather x6 -> x0, local copies, waits for them, and re-layouts: 16.6 us -> none  [the longest x3 9.56 us: to_slots(): jnp.take(array, block_of, axis=0)]
  transfers between devices with their start and end apart: 7 -> 5, of which waited for: 7 -> 3; matrix products, arithmetic and copies ran while one was open for 8% -> 19% of each run, Pallas kernels for 0% -> 17%
where the time goes in v2:
time: 545 us; the launch traced here: 543 us
  Pallas kernels  241 us (44%)
  waiting for transfers between devices  81.2 us (15%)
  other arithmetic  79.9 us (15%)
  between operations  45.1 us (8%)
  blocking collectives  38.6 us (7%)
  local copies, waits for them, and re-layouts  31.6 us (6%)
  matrix products  21.2 us (4%)
    pallas_call x2, Pallas kernels, gather_ring(): pl.pallas_call(functools.partial(gather_kernel, n, shared), out_shape=jax...  186 us
    all_gather x1, waiting for transfers between devices, gather_rows(): return lax.all_gather(part, ('dp', 'core'), axis=1, tiled=True)  67.3 us
    pallas_call x1, Pallas kernels, sum_rows(): pl.pallas_call(functools.partial(sum_kernel, n, rows), out_shape=jax.Shap...  55 us
    unnamed x45, other arithmetic  50.6 us
    psum x1, blocking collectives, per_device(): lax.psum(jnp.concatenate([jnp.pad(adam_part, (0, padded - count)), dir_pa...  38.6 us
    dot_general x3, matrix products, dot(): lax.dot_general(a, b, (dims, ((0,), (0,))), preferred_element_type=jnp.fl...  21.2 us
  transfers between devices with their start and end apart: 5, of which 3 were waited for; matrix products, arithmetic and copies ran while one was open for 19% of the time, Pallas kernels for 17%

profile of v2, /device:TPU:0, one launch (start us, length us, event | category | flops | bytes accessed | tf_op | source)
XLA Modules:
  0.0 543.4 jit_solution(2580039903443979770)
XLA Ops:
  7.2 2.5 copy-done
  9.7 55.0 %sum_ring.1 = bf16[10,128,256]{2,1,0:T(8,128)(2,1)} custom-call(bf16[10,1024,256]{2,1,0:T(8,128)(2,1)S(1)} %bitcast.183), custom_call_target="tpu_custom_call" | custom-call | bytes 200000000 | tf_op jit(solution)/shard_map/sum_ring/pallas_call | solution.py:106
  119.2 2.9 pad_maximum_fusion
  122.1 4.1 copy.41
  128.3 95.0 %gather_ring_1.1 = bf16[5,1024,1024]{2,1,0:T(8,128)(2,1)} custom-call(bf16[5,64,1024]{2,1,0:T(8,128)(2,1)} %constant_dynamic-slice_fusion.x_ref), custom_call_target="tpu_custom_call" | custom-call | bytes 200000000 | tf_op jit(solution)/shard_map/gather_ring_1/pallas_call | solution.py:185
  223.4 6.9 %fusion.13 = bf16[1,5,64,1024]{3,2,1,0:T(8,128)(2,1)S(1)} fusion(bf16[5,1024,1024]{2,1,0:T(8,128)(2,1)} %gather_ring_1.1, s32[]{:T(128)S(6)} %select_n.648), kind=kOutput, calls=%fused_computation.29 | convolution fusion | flops 671416320 | bytes 12451844 | tf_op jit(solution)/shard_map/dot_general | solution.py:204
  230.9 3.3 fusion.12
  235.6 2.1 unstack.23
  261.7 4.0 fusion.10
  265.8 9.4 %all-gather.8.cloned.1.call-done = bf16[8,5,64,1024]{3,2,1,0:T(8,128)(2,1)} async-done(((bf16[2,5,64,1024]{3,2,1,0:T(8,128)(2,1)}), bf16[8,5,64,1024]{3,2,1,0:T(8,128)(2,1)}) %all-gather.8.cloned.1.call-update) | async-done | bytes 5242896 | tf_op jit(solution)/shard_map/all_gather | solution.py:264
  275.2 3.2 copy.43
  291.5 2.2 convert_add_fusion
  294.4 3.8 fusion.6
  298.2 67.3 %all-gather.10.cloned.1.call-done = bf16[1,5,1024,1024]{3,2,1,0:T(8,128)(2,1)} async-done(((bf16[1,5,64,1024]{3,2,1,0:T(8,128)(2,1)}), bf16[1,5,1024,1024]{3,2,1,0:T(8,128)(2,1)}) %all-gather.10.cloned.1.call-update) | async-done | bytes 10485776 | tf_op jit(solution)/shard_map/all_gather | solution.py:200
  365.4 11.0 %multiply_reduce_fusion.1 = (f32[5]{0:T(128)S(1)}, f32[5,64,1024]{2,1,0:T(8,128)S(1)}) fusion(bf16[1,5,1024,1024]{3,2,1,0:T(8,128)(2,1)} %all-gather.10.cloned.1.call-done, bf16[5,1024,1024]{2,1,0:T(8,128)(2,1)} %gather_ring_1.1, bf16[1,15,64,1024]{3,2,1,0:T(8,128)(2,1)} %reduce-scatter.2.cloned.1.call-done), kind=kOutput, calls=%fused_computation.26 | convolution fusion | flops 1343160320 | bytes 22937620 | tf_op jit(solution)/shard_map/dot_general | solution.py:204
  376.7 2.3 bitcast_dynamic-update-slice_fusion.43
  379.1 38.6 %psum.7 = f32[20]{0:T(128)S(1)} all-reduce(f32[20]{0:T(128)S(1)} %pad_maximum_fusion.2), channel_id=1, replica_groups=mesh['dp'=8,'y'=2,'core'=2] {'dp','y','core'}, use_global_device_ids=true, to_apply=%region_7.8 | all-reduce | flops 20 | bytes 160 | tf_op jit(solution)/shard_map/psum | solution.py:286
  419.3 2.6 broadcast_in_dim_reshape.3
  423.9 4.2 all-to-all-start
  428.1 2.4 bitcast_dynamic-update-slice_fusion.42
  430.5 3.6 convert_add_fusion.1
  434.1 4.3 all-to-all-done
  440.4 91.3 %gather_ring_2.1 = bf16[10,1024,256]{2,1,0:T(8,128)(2,1)} custom-call(bf16[10,128,256]{2,1,0:T(8,128)(2,1)} %bitcast.201), custom_call_target="tpu_custom_call" | custom-call | bytes 200000000 | tf_op jit(solution)/shard_map/gather_ring_2/pallas_call | solution.py:185
  531.7 5.2 copy.93
  (113 shorter events, 71.1 us)
Async XLA Ops:
  7.2 119.2 %all-gather.6.cloned.1.call-start = ((), (), s32[]{:S(2)}) async-start(), calls=%async_computation.2 | async-start | bytes 3276800 | tf_op jit(solution)/shard_map/all_gather | solution.py:254
  7.2 2.5 copy-start
  9.7 55.1 %copy-start.15 = (s32[10]{0:T(128)S(1)}, s32[10]{0:T(128)}, u32[]{:S(2)}) copy-start(s32[10]{0:T(128)} %param.10) | copy-start | bytes 124
  9.7 60.6 %copy-start.7 = (bf16[1,6,128,1024]{3,2,1,0:T(8,128)(2,1)S(1)}, bf16[1,6,128,1024]{3,2,1,0:T(8,128)(2,1)}, u32[]{:S(2)}) copy-start(bf16[1,6,128,1024]{3,2,1,0:T(8,128)(2,1)} %param.13) | copy-start | bytes 4718596
  9.7 60.6 %copy-start.8 = (bf16[1,6,128,1024]{3,2,1,0:T(8,128)(2,1)S(1)}, bf16[1,6,128,1024]{3,2,1,0:T(8,128)(2,1)}, u32[]{:S(2)}) copy-start(bf16[1,6,128,1024]{3,2,1,0:T(8,128)(2,1)} %param.15) | copy-start | bytes 4718596
  64.7 170.9 %reduce-scatter.2.cloned.1.call-start = ((), (), s32[]{:S(2)}) async-start(), calls=%async_computation.3 | async-start | bytes 9830400 | tf_op jit(solution)/shard_map/reduce_scatter | solution.py:247
  98.2 14.0 %copy-start.9 = (bf16[1,6,128,1024]{3,2,1,0:T(8,128)(2,1)S(1)}, bf16[1,6,128,1024]{3,2,1,0:T(8,128)(2,1)}, u32[]{:S(2)}) copy-start(bf16[1,6,128,1024]{3,2,1,0:T(8,128)(2,1)} %param.14) | copy-start | bytes 4718596
  112.1 7.1 %copy-start.11 = (bf16[10,128,1024]{2,1,0:T(8,128)(2,1)S(1)}, bf16[10,128,1024]{2,1,0:T(8,128)(2,1)}, u32[]{:S(2)}) copy-start(bf16[10,128,1024]{2,1,0:T(8,128)(2,1)} %bitcast_dynamic-update-slice_fusion) | copy-start | bytes 7864324
  126.3 149.0 %all-gather.8.cloned.1.call-start = ((), (), s32[]{:S(2)}) async-start(), calls=%async_computation.4 | async-start | bytes 6553600 | tf_op jit(solution)/shard_map/all_gather | solution.py:264
  223.4 7.4 %copy-start.1 = (bf16[5,1024,1024]{2,1,0:T(8,128)(2,1)S(1)}, bf16[5,1024,1024]{2,1,0:T(8,128)(2,1)}, u32[]{:S(2)}) copy-start(bf16[5,1024,1024]{2,1,0:T(8,128)(2,1)} %gather_ring_1.1) | copy-start | bytes 31457284
  223.4 7.5 %copy-start.5 = (bf16[5,64,1024]{2,1,0:T(8,128)(2,1)S(1)}, bf16[5,64,1024]{2,1,0:T(8,128)(2,1)}, u32[]{:S(2)}) copy-start(bf16[5,64,1024]{2,1,0:T(8,128)(2,1)} %constant_dynamic-slice_fusion.x_ref) | copy-start | bytes 1966084
  235.4 26.3 %copy-start.2 = (f32[1,6,128,1024]{3,2,1,0:T(8,128)S(1)}, f32[1,6,128,1024]{3,2,1,0:T(8,128)}, u32[]{:S(2)}) copy-start(f32[1,6,128,1024]{3,2,1,0:T(8,128)} %param.17) | copy-start | bytes 9437188
  235.4 130.1 %all-gather.10.cloned.1.call-start = ((), (), s32[]{:S(2)}) async-start(), calls=%async_computation.5 | async-start | bytes 11141120 | tf_op jit(solution)/shard_map/all_gather | solution.py:200
  278.4 1.7 copy-start.6
  279.4 7.8 %copy-start.4 = (bf16[1,2,5,2,64,1024]{5,4,3,2,1,0:T(8,128)(2,1)}, bf16[1,2,5,2,64,1024]{5,4,3,2,1,0:T(8,128)(2,1)S(1)}, u32[]{:S(2)}) copy-start(bf16[1,2,5,2,64,1024]{5,4,3,2,1,0:T(8,128)(2,1)S(1)} %get-tuple-element.8) | copy-start | bytes 7864324
  283.8 7.7 %copy-start.12 = (f32[1,6,128,1024]{3,2,1,0:T(8,128)S(1)}, f32[1,6,128,1024]{3,2,1,0:T(8,128)}, u32[]{:S(2)}) copy-start(f32[1,6,128,1024]{3,2,1,0:T(8,128)} %param.12) | copy-start | bytes 9437188
  287.9 2.9 copy-start.14
  291.5 2.9 copy-start.3
  298.2 119.6 %copy-start.10 = (bf16[1,15,64,1024]{3,2,1,0:T(8,128)(2,1)S(1)}, bf16[1,15,64,1024]{3,2,1,0:T(8,128)(2,1)}, u32[]{:S(2)}) copy-start(bf16[1,15,64,1024]{3,2,1,0:T(8,128)(2,1)} %reduce-scatter.2.cloned.1.call-done) | copy-start | bytes 5898244
  419.3 11.2 %copy-start.13 = (f32[1,6,128,1024]{3,2,1,0:T(8,128)S(1)}, f32[1,6,128,1024]{3,2,1,0:T(8,128)}, u32[]{:S(2)}) copy-start(f32[1,6,128,1024]{3,2,1,0:T(8,128)} %param.11) | copy-start | bytes 9437188
  423.9 14.5 %all-to-all-start = ((bf16[1,5,64,4,256]{4,2,1,0,3:T(8,128)(2,1)}), bf16[1,5,64,4,256]{4,2,1,0,3:T(8,128)(2,1)}, u32[]{:S(2)}, u32[]{:S(2)}) async-start(bf16[1,5,64,4,256]{4,2,1,0,3:T(8,128)(2,1)} %copy.38), calls=%async_computation.1 | async-start | bytes 1310720 | tf_op jit(solution)/shard_map/all_to_all | solution.py:294
Sparse Core Ops, SparseCore 0:
  64.9 27.5 all-gather.5
  126.4 70.6 reduce-scatter.1
  235.5 39.6 all-gather.7
  277.5 87.8 all-gather.9

commit v3 on v2

--- a/solution.py
+++ b/solution.py
@@ -121,9 +121,10 @@
     )(grads)
 
 
-def gather_kernel(n, shared, x_ref, out_ref, local_sem, send_sem, recv_sem, *pair_sems):
+def gather_kernel(n, shared, x_ref, out_ref, send_sem, recv_sem, *pair_sems):
     place, way, after, before = ring(n)
-    rows = x_ref.shape[1]
+    count, rows = x_ref.shape[:2]
+    half = count // 2
     core = lax.axis_index("core")
     other = {"core": 1 - core}
     barrier = pltpu.get_barrier_semaphore()
@@ -132,50 +133,54 @@
         pl.semaphore_signal(barrier, inc=1, device_id=other, device_id_type=MESH)
     pl.semaphore_wait(barrier, 2 if shared else 1)
 
-    def spot(step):
+    def first_row(step):
         index = index_at((place - way * step + 2 * n) % n, n)
         first = (index * CORES + core) * rows if shared else index * rows
-        return out_ref.at[:, pl.ds(pl.multiple_of(first, rows), rows), :]
-
-    def copy(step, sems, target):
+        return pl.multiple_of(first, rows)
+
+    def copy(step, part, sems, target):
+        blocks = pl.ds(part * half, half if part == 0 else count - half)
+        spot = out_ref.at[blocks, pl.ds(first_row(step), rows), :]
         return pltpu.make_async_remote_copy(
-            src_ref=spot(step),
-            dst_ref=spot(step),
-            send_sem=sems[0].at[step],
-            recv_sem=sems[1].at[step],
+            src_ref=spot,
+            dst_ref=spot,
+            send_sem=sems[0].at[step, part],
+            recv_sem=sems[1].at[step, part],
             device_id=target,
             device_id_type=MESH,
         )
 
-    def onward(step):
-        return copy(step, (send_sem, recv_sem), {"dp": after})
-
-    own = pltpu.make_async_copy(x_ref, spot(0), local_sem)
-    own.start()
-    own.wait()
-    onward(0).start()
-    if shared:
-        copy(0, pair_sems, other).start()
+    def onward(step, part):
+        return copy(step, part, (send_sem, recv_sem), {"dp": after})
+
+    out_ref[:, pl.ds(first_row(0), rows), :] = x_ref[...]
+    for part in range(2):
+        onward(0, part).start()
+        if shared:
+            copy(0, part, pair_sems, other).start()
 
     @pl.loop(1, n)
     def _(step):
-        onward(step - 1).wait_recv()
-
-        @pl.when(step < n - 1)
-        def _():
-            onward(step).start()
-
-        if shared:
-            copy(step, pair_sems, other).start()
+        for part in range(2):
+            onward(step - 1, part).wait_recv()
+
+            @pl.when(step < n - 1)
+            def _():
+                onward(step, part).start()
+
+            if shared:
+                copy(step, part, pair_sems, other).start()
 
     @pl.loop(0, n)
     def _(step):
-        @pl.when(step < n - 1)
-        def _():
-            onward(step).wait_send()
-
-        if shared:
-            copy(step, pair_sems, other).wait()
+        for part in range(2):
+
+            @pl.when(step < n - 1)
+            def _():
+                onward(step, part).wait_send()
+
+            if shared:
+                copy(step, part, pair_sems, other).wait()
 
 
 def gather_ring(part, shared, number):
@@ -185,19 +190,16 @@
     return pl.pallas_call(
         functools.partial(gather_kernel, n, shared),
         out_shape=jax.ShapeDtypeStruct((count, height, width), part.dtype),
-        in_specs=[pl.BlockSpec(memory_space=pl.ANY)],
-        out_specs=pl.BlockSpec(memory_space=pl.ANY),
-        scratch_shapes=[pltpu.SemaphoreType.DMA]
-        + [pltpu.SemaphoreType.DMA((n - 1,))] * 2
-        + ([pltpu.SemaphoreType.DMA((n,))] * 2 if shared else []),
-        compiler_params=pltpu.CompilerParams(collective_id=number, has_side_effects=True),
+        in_specs=[pl.BlockSpec(memory_space=pltpu.VMEM)],
+        out_specs=pl.BlockSpec(memory_space=pltpu.VMEM),
+        scratch_shapes=[pltpu.SemaphoreType.DMA((n - 1, 2))] * 2
+        + ([pltpu.SemaphoreType.DMA((n, 2))] * 2 if shared else []),
+        compiler_params=pltpu.CompilerParams(
+            collective_id=number, has_side_effects=True, vmem_limit_bytes=24 * 2**20
+        ),
         cost_estimate=pl.CostEstimate(flops=0, bytes_accessed=200_000_000, transcendentals=0),
         name="gather_ring_%d" % number,
     )(part)
-
-
-def gather_rows(part):
-    return lax.all_gather(part, ("dp", "core"), axis=1, tiled=True)
 
 
 def dot(a, b, dims):
@@ -239,18 +241,17 @@
         ])
         return jnp.pad(picked, ((0, padded - count), (0, 0), (0, 0)))
 
-    def to_plane(arrays):
+    def to_send(arrays):
         picked = jnp.stack([by_block(array) for array in arrays])
         kinds = len(arrays)
         picked = picked.reshape(kinds, planes, per_plane, CORES, part, width)
-        picked = picked.transpose(1, 3, 0, 2, 4, 5).reshape(-1, kinds * per_plane, part, width)
-        out = lax.psum_scatter(picked, GRID, scatter_dimension=0, tiled=True)
-        return out.reshape(kinds, per_plane, part, width)
-
-    rroot, lroot, weight = to_plane((right_root, left_root, weights))
-    rroot_all = gather_rows(rroot)
-
-    reduced = sum_rows(grads[0])
+        return picked.transpose(1, 3, 0, 2, 4, 5).reshape(-1, kinds * per_plane, part, width)
+
+    picked, terms = lax.optimization_barrier((to_send((right_root, left_root, weights)), grads[0]))
+    placed = lax.psum_scatter(picked, GRID, scatter_dimension=0, tiled=True)
+
+    reduced, placed = lax.optimization_barrier((sum_rows(terms), placed))
+    rroot, lroot, weight = placed.reshape(-1, per_plane, part, width)
     summed = lax.all_gather(reduced, GRID, axis=2, tiled=True)
     wide = jnp.pad(summed, ((0, padded - count), (0, 0), (0, 0)))
     own = lax.dynamic_slice(wide, (y * per_plane, core * part, 0), (per_plane, part, width))
@@ -261,7 +262,9 @@
     half = dot(lroot, full, ((2,), (1,))).astype(jnp.bfloat16)
     left_inc = dot(own, full, ((2,), (2,))).astype(jnp.bfloat16)
     right_inc = dot(own_cols, full, ((1,), (1,))).astype(jnp.bfloat16)
-    incs = lax.all_gather(jnp.stack([left_inc, right_inc]), GRID)
+    incs, rroot = lax.optimization_barrier((jnp.stack([left_inc, right_inc]), rroot))
+    rroot_all = gather_ring(rroot, True, 3)
+    incs = lax.all_gather(incs, GRID)
     incs = incs.reshape(planes, CORES, 2, per_plane, part, width)
     incs = incs.transpose(2, 0, 3, 1, 4, 5).reshape(2, padded, rows, width)
 

time: 545 us -> 491 us (0.901)
  waiting for transfers between devices: 81.2 us -> 40.4 us
  Pallas kernels: 241 us -> 219 us
  other arithmetic: 79.9 us -> 92.5 us
    all_gather x2 -> x1, waiting for transfers between devices: 76.7 us -> 0.01 us  [per_device(): incs = lax.all_gather(incs, GRID)]
    all_gather x1, waiting for transfers between devices: 0.02 us -> 26.1 us  [per_device(): summed = lax.all_gather(reduced, GRID, axis=2, tiled=True)]
    pallas_call x2 -> x3, Pallas kernels: 186 us -> 164 us  [gather_ring(): pl.pallas_call(functools.partial(gather_kernel, n, shared), out_shape=jax...]
    reduce_scatter x1, waiting for transfers between devices: 0.02 us -> 14.3 us  [per_device(): placed = lax.psum_scatter(picked, GRID, scatter_dimension=0, tiled=True)]
    unnamed x45 -> x47, other arithmetic: 50.6 us -> 60.8 us
    unnamed x33 -> x29, local copies, waits for them, and re-layouts: 9.68 us -> 12.5 us
  transfers between devices with their start and end apart: 5 -> 4, of which waited for: 3 -> 2; matrix products, arithmetic and copies ran while one was open for 19% -> 11% of each run, Pallas kernels for 17% -> 33%
where the time goes in v3:
time: 491 us; the launch traced here: 489 us
  Pallas kernels  219 us (45%)
  other arithmetic  92.5 us (19%)
  between operations  44.7 us (9%)
  waiting for transfers between devices  40.4 us (8%)
  blocking collectives  39 us (8%)
  local copies, waits for them, and re-layouts  31.4 us (6%)
  matrix products  17.6 us (4%)
    pallas_call x3, Pallas kernels, gather_ring(): pl.pallas_call(functools.partial(gather_kernel, n, shared), out_shape=jax...  164 us
    unnamed x47, other arithmetic  60.8 us
    pallas_call x1, Pallas kernels, sum_rows(): pl.pallas_call(functools.partial(sum_kernel, n, rows), out_shape=jax.Shap...  55 us
    psum x1, blocking collectives, per_device(): lax.psum(jnp.concatenate([jnp.pad(adam_part, (0, padded - count)), dir_pa...  39 us
    all_gather x1, waiting for transfers between devices, per_device(): summed = lax.all_gather(reduced, GRID, axis=2, tiled=True)  26.1 us
    dot_general x3, matrix products, dot(): lax.dot_general(a, b, (dims, ((0,), (0,))), preferred_element_type=jnp.fl...  17.6 us
    reduce_scatter x1, waiting for transfers between devices, per_device(): placed = lax.psum_scatter(picked, GRID, scatter_dimension=0, tiled=True)  14.3 us
    unnamed x29, local copies, waits for them, and re-layouts  12.5 us
  transfers between devices with their start and end apart: 4, of which 2 were waited for; matrix products, arithmetic and copies ran while one was open for 11% of the time, Pallas kernels for 33%

profile of v3, /device:TPU:0, one launch (start us, length us, event | category | flops | bytes accessed | tf_op | source)
XLA Modules:
  0.0 488.9 jit_solution(10630401897145918853)
XLA Ops:
  24.1 2.6 bitcast_dynamic-update-slice_fusion.27
  31.9 2.3 bitcast_dynamic-update-slice_fusion.35
  34.2 2.3 bitcast_dynamic-update-slice_fusion.25
  70.1 3.5 pad_maximum_fusion
  73.6 4.0 copy.41
  77.7 2.5 copy-done.3
  80.2 55.0 %sum_ring.1 = bf16[10,128,256]{2,1,0:T(8,128)(2,1)} custom-call(bf16[10,1024,256]{2,1,0:T(8,128)(2,1)S(1)} %bitcast.180), custom_call_target="tpu_custom_call" | custom-call | bytes 200000000 | tf_op jit(solution)/shard_map/sum_ring/pallas_call | solution.py:106
  135.2 14.3 %reduce-scatter.2.cloned.1.call-done = bf16[1,15,64,1024]{3,2,1,0:T(8,128)(2,1)} async-done(((bf16[4,15,64,1024]{3,2,1,0:T(8,128)(2,1)}), bf16[1,15,64,1024]{3,2,1,0:T(8,128)(2,1)}) %reduce-scatter.2.cloned.1.call-update) | async-done | bytes 1966096 | tf_op jit(solution)/shard_map/reduce_scatter | solution.py:251
  150.9 26.1 %all-gather.4.cloned.1.call-done = bf16[10,128,1024]{2,1,0:T(8,128)(2,1)} async-done(((bf16[10,128,256]{2,1,0:T(8,128)(2,1)}), bf16[10,128,1024]{2,1,0:T(8,128)(2,1)}) %all-gather.4.cloned.1.call-update) | async-done | bytes 2621456 | tf_op jit(solution)/shard_map/all_gather | solution.py:255
  178.2 55.6 %gather_ring_1.1 = bf16[5,1024,1024]{2,1,0:T(8,128)(2,1)S(1)} custom-call(bf16[5,64,1024]{2,1,0:T(8,128)(2,1)S(1)} %constant_dynamic-slice_fusion.x_ref), custom_call_target="tpu_custom_call" | custom-call | bytes 200000000 | tf_op jit(solution)/shard_map/gather_ring_1/pallas_call | solution.py:190
  233.8 3.3 fusion.10
  237.7 2.4 fusion.11
  254.8 54.7 %gather_ring_3.1 = bf16[5,1024,1024]{2,1,0:T(8,128)(2,1)S(1)} custom-call(bf16[5,64,1024]{2,1,0:T(8,128)(2,1)S(1)} %slice_bitcast_fusion.x_ref), custom_call_target="tpu_custom_call" | custom-call | bytes 200000000 | tf_op jit(solution)/shard_map/gather_ring_3/pallas_call | solution.py:190
  309.5 3.8 copy-done.1
  313.4 12.0 %multiply_reduce_fusion.1 = (f32[5]{0:T(128)S(1)}, f32[5,64,1024]{2,1,0:T(8,128)}) fusion(bf16[5,1024,1024]{2,1,0:T(8,128)(2,1)} %copy-done.1, bf16[5,1024,1024]{2,1,0:T(8,128)(2,1)} %copy-done, bf16[1,15,64,1024]{3,2,1,0:T(8,128)(2,1)} %reduce-scatter.2.cloned.1.call-done), kind=kOutput, calls=%fused_computation.24 | convolution fusion | flops 1343160320 | bytes 22937620 | tf_op jit(solution)/shard_map/dot_general | solution.py:206
  335.5 4.0 fusion.8
  339.6 39.0 %psum.7 = f32[20]{0:T(128)S(1)} all-reduce(f32[20]{0:T(128)S(1)} %pad_maximum_fusion.2), channel_id=1, replica_groups=mesh['dp'=8,'y'=2,'core'=2] {'dp','y','core'}, use_global_device_ids=true, to_apply=%region_7.8 | all-reduce | flops 20 | bytes 160 | tf_op jit(solution)/shard_map/psum | solution.py:289
  382.9 2.5 broadcast_in_dim_reshape.3
  387.4 4.2 all-to-all-start
  401.6 3.8 fusion.4
  406.5 53.5 %gather_ring_2.1 = bf16[10,1024,256]{2,1,0:T(8,128)(2,1)S(1)} custom-call(bf16[10,128,256]{2,1,0:T(8,128)(2,1)S(1)} %bitcast.181), custom_call_target="tpu_custom_call" | custom-call | bytes 200000000 | tf_op jit(solution)/shard_map/gather_ring_2/pallas_call | solution.py:190
  460.0 2.3 copy-done.2
  462.3 3.2 copy.43
  480.0 2.4 copy.93
  (109 shorter events, 85.0 us)
Async XLA Ops:
  7.2 30.0 %copy-start.7 = (bf16[1,6,128,1024]{3,2,1,0:T(8,128)(2,1)S(1)}, bf16[1,6,128,1024]{3,2,1,0:T(8,128)(2,1)}, u32[]{:S(2)}) copy-start(bf16[1,6,128,1024]{3,2,1,0:T(8,128)(2,1)} %param.13) | copy-start | bytes 4718596
  7.2 31.4 %copy-start.8 = (bf16[1,6,128,1024]{3,2,1,0:T(8,128)(2,1)S(1)}, bf16[1,6,128,1024]{3,2,1,0:T(8,128)(2,1)}, u32[]{:S(2)}) copy-start(bf16[1,6,128,1024]{3,2,1,0:T(8,128)(2,1)} %param.15) | copy-start | bytes 4718596
  7.2 142.3 %reduce-scatter.2.cloned.1.call-start = ((), (), s32[]{:S(2)}) async-start(), calls=%async_computation.2 | async-start | bytes 9830400 | tf_op jit(solution)/shard_map/reduce_scatter | solution.py:251
  57.7 7.6 %copy-start.9 = (bf16[1,6,128,1024]{3,2,1,0:T(8,128)(2,1)S(1)}, bf16[1,6,128,1024]{3,2,1,0:T(8,128)(2,1)}, u32[]{:S(2)}) copy-start(bf16[1,6,128,1024]{3,2,1,0:T(8,128)(2,1)} %param.14) | copy-start | bytes 4718596
  77.6 99.4 %all-gather.4.cloned.1.call-start = ((), (), s32[]{:S(2)}) async-start(), calls=%async_computation.3 | async-start | bytes 3276800 | tf_op jit(solution)/shard_map/all_gather | solution.py:255
  77.7 2.5 copy-start.3
  149.5 312.8 %all-gather.6.cloned.1.call-start = ((), (), s32[]{:S(2)}) async-start(), calls=%async_computation.4 | async-start | bytes 6553600 | tf_op jit(solution)/shard_map/all_gather | solution.py:267
  233.8 4.0 copy-start
  309.5 3.8 copy-start.1
  325.3 10.1 %copy-start.4 = (f32[1,6,128,1024]{3,2,1,0:T(8,128)S(1)}, f32[1,6,128,1024]{3,2,1,0:T(8,128)}, u32[]{:S(2)}) copy-start(f32[1,6,128,1024]{3,2,1,0:T(8,128)} %param.17) | copy-start | bytes 9437188
  378.6 2.1 copy-start.6
  387.4 17.9 %all-to-all-start = ((bf16[1,5,64,4,256]{4,2,1,0,3:T(8,128)(2,1)}), bf16[1,5,64,4,256]{4,2,1,0,3:T(8,128)(2,1)}, u32[]{:S(2)}, u32[]{:S(2)}) async-start(bf16[1,5,64,4,256]{4,2,1,0,3:T(8,128)(2,1)} %copy.38), calls=%async_computation.1 | async-start | bytes 1310720 | tf_op jit(solution)/shard_map/all_to_all | solution.py:297
  391.6 10.0 %copy-start.5 = (f32[1,6,128,1024]{3,2,1,0:T(8,128)S(1)}, f32[1,6,128,1024]{3,2,1,0:T(8,128)}, u32[]{:S(2)}) copy-start(f32[1,6,128,1024]{3,2,1,0:T(8,128)} %param.16) | copy-start | bytes 9437188
  460.0 2.4 copy-start.2
  467.8 7.0 %copy-start.10 = (f32[1,6,128,1024]{3,2,1,0:T(8,128)S(1)}, f32[1,6,128,1024]{3,2,1,0:T(8,128)}, u32[]{:S(2)}) copy-start(f32[1,6,128,1024]{3,2,1,0:T(8,128)} %param.12) | copy-start | bytes 9437188
  474.8 2.8 copy-start.11
  474.8 5.0 %slice-start = ((s8[5242880]{0:T(1024)(128)(4,1)}), s8[4194304]{0:T(1024)(128)(4,1)S(1)}, s32[]{:S(2)}) async-start(s8[5242880]{0:T(1024)(128)(4,1)} %bitcast.178), calls=%async_computation.5 | async-start | bytes 8388608
  477.6 2.3 slice-start.1
Sparse Core Ops, SparseCore 0:
  77.8 71.6 reduce-scatter.1
  151.1 25.8 all-gather.3
  241.4 39.8 all-gather.5
